TPU v7x, 32 devices: a whole 2x2x4 slice. The times are simulated.
32 devices in a mesh: slides: 2 (over y), rows: 4 (over z), cols: 2 (over x), chan: 2 (over core).
Axes of the slice: x: 2, y: 2, z: 4, core: 2. Of those that a mesh axis runs over, the one named last changes fastest.
Arguments:
- features: bfloat16 [128, 64, 384], P(('slides', 'rows'), 'cols', 'chan'), parts along dimension 0, may hold values from -6 to 6
- gate_input: bfloat16 [128, 64, 384], P(('slides', 'rows'), 'cols', 'chan'), parts along dimension 0, may hold values from -6 to 6
- decay_idx: int32 [128, 64], P(('slides', 'rows'), 'cols'), parts along dimension 0, may hold values from 0 to 15
- log_table: float32 [16, 384], P(None, 'chan'), may hold values from -1 to 0, as said below
- state_rate: float32 [16], replicated, may hold values from 0.5 to 2
- proj_row: bfloat16 [384, 32], P('chan'), may hold values from -0.0390625 to 0.0390625
- proj_col: bfloat16 [384, 32], P('chan'), may hold values from -0.0390625 to 0.0390625
- conv_w: float32 [3, 3, 384], P(None, None, 'chan'), may hold values from -0.5 to 0.5
- conv_b: float32 [384], P('chan'), may hold values from -0.5 to 0.5
- d_skip: float32 [384], P('chan'), may hold values from 0.5 to 1.5
Outputs:
- output: bfloat16 [128, 64, 384], P(('slides', 'rows'), 'cols', 'chan'), parts along dimension 0
There are 2 independent parts, one for each index of `slides`. A program takes and returns all parts, laid end to end along the dimension named above; an argument that names none is the same for every part. Nothing has to cross between parts.
Inputs may be any that keep to these rules, and one draw needn't show every extreme that they name: `log_table`: every entry is negative.
All inputs are finite; a program needn't handle non-finite values.
Results may differ from a plain program's by a relative error of at most 0.0061.
Values may be sent and summed in bfloat16 or wider, within the bound.
A program may use at most 128 MiB of HBM per device.

v0:
```python
import jax
import jax.numpy as jnp
from jax import lax
from jax.sharding import PartitionSpec as P


def entering(shard, axis, combine, identity):
    size, position = (lax.axis_size(axis), lax.axis_index(axis))
    everything = jax.tree.map(lambda part: lax.all_gather(part, axis), shard)
    start = jax.tree.map(
        lambda part, zero: jnp.broadcast_to(jnp.asarray(zero, part.dtype), part.shape),
        shard,
        identity,
    )

    def step(k, before):
        reached = k < position
        new = combine(before, jax.tree.map(lambda part: part[k], everything))
        return jax.tree.map(lambda a, b: jnp.where(reached, a, b), new, before)

    return lax.fori_loop(0, size, step, start)


def extended(block, sides, width):
    for axis, dim in sides:
        count = lax.axis_size(axis)
        forward = [(i, i + 1) for i in range(count - 1)]
        backward = [(target, source) for source, target in forward]
        low = lax.ppermute(
            lax.slice_in_dim(block, block.shape[dim] - width, None, axis=dim), axis, forward
        )
        high = lax.ppermute(lax.slice_in_dim(block, 0, width, axis=dim), axis, backward)
        block = jnp.concatenate([low, block, high], axis=dim)
    return block


def combine_pair(earlier, latter):
    return (earlier[0] + latter[0], latter[1] + jnp.exp(latter[0]) * earlier[1])


def make_carry_combine(state_rate):
    rates = state_rate[:, None, None]

    def combine_carry(earlier, latter):
        return (earlier[0] + latter[0], latter[1] + jnp.exp(rates * latter[0][None]) * earlier[1])

    return combine_carry


def lookup(decay_idx, log_table):
    entries = log_table.shape[0]
    onehot = (decay_idx[..., None] == jnp.arange(entries, dtype=jnp.int32)).astype(jnp.float32)
    return jnp.einsum("hwk,ke->hwe", onehot, log_table, precision=lax.Precision.HIGHEST)


def tile_states(values, log_decays, coeffs, state_rate, scan_axis):
    num_states = state_rate.shape[0]
    drive_cols = jnp.moveaxis(coeffs[..., :num_states], -1, 0)[..., None]
    log_sums = jnp.cumsum(log_decays, axis=scan_axis)

    def one_state(inputs):
        state_scale, drive_col = inputs
        unused, states = lax.associative_scan(
            combine_pair, (log_decays * state_scale, drive_col * values), axis=scan_axis
        )
        return states

    return (log_sums, lax.map(one_state, (state_rate, drive_cols)))


def finish(log_sums, states, inflow, coeffs, state_rate):
    num_states = states.shape[0]
    outputs = jnp.moveaxis(coeffs[..., num_states:], -1, 0)[..., None]
    carried = jnp.exp(state_rate[:, None, None, None] * log_sums[None]) * inflow
    return jnp.sum(outputs * (states + carried), axis=0)


def column_coeffs(middle, proj_col):
    return lax.psum(jnp.dot(middle, proj_col, preferred_element_type=jnp.float32), "chan")


def shards(
    features,
    gate_input,
    decay_idx,
    log_table,
    state_rate,
    proj_row,
    proj_col,
    conv_w,
    conv_b,
    d_skip,
):
    combine_carry = make_carry_combine(state_rate)
    log_decays = lookup(decay_idx, log_table)
    feats_wide = features.astype(jnp.float32)
    coeff_row = lax.psum(jnp.dot(features, proj_row, preferred_element_type=jnp.float32), "chan")
    row_sums, states = tile_states(feats_wide, log_decays, coeff_row, state_rate, 1)
    tile_ends = (row_sums[:, -1, :], states[:, :, -1, :])
    incoming = entering(
        tile_ends,
        "cols",
        combine_carry,
        (jnp.zeros_like(tile_ends[0]), jnp.zeros_like(tile_ends[1])),
    )
    swept_rows = finish(row_sums, states, incoming[1][:, :, None, :], coeff_row, state_rate)
    row_out = (swept_rows + d_skip * feats_wide).astype(jnp.bfloat16)
    padded = extended(row_out, (("rows", 0), ("cols", 1)), 1).astype(jnp.float32)
    tile_rows = row_out.shape[0]
    tile_cols = row_out.shape[1]
    convolved = jnp.zeros(row_out.shape, jnp.float32) + conv_b
    for offset_row in range(3):
        for offset_col in range(3):
            convolved = (
                convolved
                + conv_w[offset_row, offset_col]
                * padded[offset_row : offset_row + tile_rows, offset_col : offset_col + tile_cols]
            )
    middle = jax.nn.silu(convolved).astype(jnp.bfloat16)
    strip_vals = lax.all_to_all(middle, "rows", split_axis=1, concat_axis=0, tiled=True)
    strip_index = lax.all_to_all(decay_idx, "rows", split_axis=1, concat_axis=0, tiled=True)
    strip_decays = lookup(strip_index, log_table)
    strip_wide = strip_vals.astype(jnp.float32)
    coeff_col = column_coeffs(strip_vals, proj_col)
    col_sums, states = tile_states(strip_wide, strip_decays, coeff_col, state_rate, 0)
    strip_out = (
        finish(col_sums, states, jnp.zeros((), jnp.float32), coeff_col, state_rate)
        + d_skip * strip_wide
    )
    combined = lax.all_to_all(strip_out, "rows", split_axis=0, concat_axis=1, tiled=True)
    return (combined * jax.nn.silu(gate_input.astype(jnp.float32))).astype(jnp.bfloat16)


def solution(mesh):
    placed = (
        P(("slides", "rows"), "cols", "chan"),
        P(("slides", "rows"), "cols", "chan"),
        P(("slides", "rows"), "cols"),
        P(None, "chan"),
        P(),
        P("chan", None),
        P("chan", None),
        P(None, None, "chan"),
        P("chan"),
        P("chan"),
    )
    return jax.shard_map(
        shards,
        mesh=mesh,
        in_specs=placed,
        out_specs=P(("slides", "rows"), "cols", "chan"),
        check_vma=False,
    )
```

profile of v0, /device:TPU:24, one launch (start us, length us, event | category | flops | bytes accessed | tf_op | source)
XLA Modules:
  0.0 395.9 jit_solution(8053558625621068115)
XLA Ops:
  6.5 1.9 fusion.42
  9.9 5.1 %all-to-all-start.1 = ((s32[4,1,128]{2,1,0:T(1,128)}), s32[4,1,128]{2,1,0:T(1,128)S(1)}, u32[]{:S(2)}, u32[]{:S(2)}) async-start(s32[4,1,128]{2,1,0:T(1,128)} %reshape.23), calls=%async_computation.1 | async-start | bytes 4096 | tf_op jit(solution)/shard_map/all_to_all | solution.py:121
  15.0 1.1 fusion.36
  16.5 1.8 convert_element_type.23
  18.3 1.2 copy.49
  19.5 4.4 %all-gather.1 = f32[32,1,192]{2,0,1:T(8,128)S(1)} all-gather(f32[16,1,192]{2,0,1:T(8,128)S(1)} %slice.400), channel_id=3, replica_groups=mesh['slides'=2,'rows'=4,'cols'=2,'chan'=2] {'cols'}, dimensions={0}, use_global_device_ids=true | all-gather | bytes 36864 | tf_op jit(solution)/shard_map/all_gather | solution.py:9
  23.9 5.3 %all-reduce.25.cloned.1.call-done = f32[16,32,32]{2,1,0:T(8,128)} async-done(((f32[16,32,32]{2,1,0:T(8,128)}), f32[16,32,32]{2,1,0:T(8,128)}) %all-reduce.25.cloned.1.call-update) | async-done | bytes 65552 | tf_op jit(solution)/shard_map/psum | solution.py:97
  29.2 1.9 slice_bitcast_fusion.3
  31.9 179.7 %while.37 = (s32[]{:T(128)}, f32[16,16,32,192]{3,2,1,0:T(8,128)}, f32[16,16,32,1]{2,1,3,0:T(8,128)}, f32[16,32,192]{2,1,0:T(8,128)}, f32[16]{0:T(128)}, /*index=5*/f32[16,32,192]{2,1,0:T(8,128)S(1)}) while((s32[]{:T(128)}, f32[16,16,32,192]{3,2,1,0:T(8,128)}, f32[16,16,32,1]{2,1,3,0:T(8,128)}, f32[16,32,192]{2,1,0:T(8,128)}, ...), condition=%wide.region_2.3_spmd.clone, body=%wide.region_1.0_spmd.sunk.clone | while | flops 998402 | bytes 15030905 | solution.py:68
  32.6 1.3 dynamic_slice.48
  33.9 1.9 broadcast_multiply_fusion.8
  42.2 0.9 bitcast_dynamic-update-slice_fusion.6
  43.8 1.3 dynamic_slice.48
  45.1 1.9 broadcast_multiply_fusion.8
  53.5 0.9 bitcast_dynamic-update-slice_fusion.6
  55.0 1.3 dynamic_slice.48
  56.3 1.9 broadcast_multiply_fusion.8
  66.3 1.3 dynamic_slice.48
  67.6 1.9 broadcast_multiply_fusion.8
  77.5 1.3 dynamic_slice.48
  78.8 1.9 broadcast_multiply_fusion.8
  88.7 1.3 dynamic_slice.48
  90.0 1.9 broadcast_multiply_fusion.8
  99.9 1.3 dynamic_slice.48
  101.2 1.9 broadcast_multiply_fusion.8
  111.1 1.3 dynamic_slice.48
  112.4 1.9 broadcast_multiply_fusion.8
  122.4 1.3 dynamic_slice.48
  123.7 1.9 broadcast_multiply_fusion.8
  133.6 1.3 dynamic_slice.48
  134.9 1.9 broadcast_multiply_fusion.8
  144.8 1.3 dynamic_slice.48
  146.1 1.9 broadcast_multiply_fusion.8
  156.0 1.3 dynamic_slice.48
  157.3 1.9 broadcast_multiply_fusion.8
  167.3 1.3 dynamic_slice.48
  168.6 1.9 broadcast_multiply_fusion.8
  178.5 1.3 dynamic_slice.48
  179.8 1.9 broadcast_multiply_fusion.8
  189.7 1.3 dynamic_slice.48
  191.0 1.9 broadcast_multiply_fusion.8
  200.9 1.3 dynamic_slice.48
  202.2 1.9 broadcast_multiply_fusion.8
  210.6 0.9 bitcast_dynamic-update-slice_fusion.6
  211.5 9.9 %copy.50 = f32[16,16,32,192]{3,1,2,0:T(8,128)S(1)} copy(f32[16,16,32,192]{3,2,1,0:T(8,128)} %get-tuple-element.178) | data formatting | bytes 12582912 | tf_op jit(solution)/shard_map/while | solution.py:68
  221.5 9.5 %all-gather = f32[32,16,1,192]{3,1,2,0:T(8,128)S(1)} all-gather(f32[16,16,1,192]{3,1,2,0:T(8,128)S(1)} %slice.399), channel_id=2, replica_groups=mesh['slides'=2,'rows'=4,'cols'=2,'chan'=2] {'cols'}, dimensions={0}, use_global_device_ids=true | all-gather | bytes 589824 | tf_op jit(solution)/shard_map/all_gather | solution.py:9
  231.6 4.8 %multiply_reduce_fusion.1 = f32[16,32,192]{2,1,0:T(8,128)S(1)} fusion(f32[16,16,32,192]{3,2,1,0:T(8,128)} %get-tuple-element.178, f32[16,16,192]{2,1,0:T(8,128)S(1)} %get-tuple-element.179, f32[16,32,192]{2,1,0:T(8,128)S(1)} %copy-done.4, f32[16]{0:T(128)S(1)} %bitcast.166, f32[16,16,32]{2,1,0:T(8,128)S(1)} %copy.46), kind=kLoop, calls=%fused_computation.70 | loop fusion | flops 7766016 | bytes 7307328 | tf_op jit(solution)/shard_map/reduce_sum | solution.py:75
  236.5 1.3 collective-permute-start
  237.8 4.5 %collective-permute-start.1 = (bf16[1,32,192]{2,1,0:T(8,128)(2,1)S(1)}, bf16[1,32,192]{2,1,0:T(8,128)(2,1)S(1)}, u32[]{:S(2)}, u32[]{:S(2)}) collective-permute-start(bf16[1,32,192]{2,1,0:T(8,128)(2,1)S(1)} %get-tuple-element.320), channel_id=1, source_target_pairs={{4,0},{8,4},{12,8},{5,1},{9,5},{13,9},{6,2},{10,6},{14,10},{7,3},{... | collective-permute-start | bytes 36872 | tf_op jit(solution)/shard_map/ppermute | solution.py:32
  243.8 3.4 collective-permute-start.2
  247.2 1.3 collective-permute-start.3
  248.6 4.2 %collective-permute-done.3 = bf16[18,1,192]{2,1,0:T(2,128)(2,1)S(1)} collective-permute-done((bf16[18,1,192]{2,1,0:T(2,128)(2,1)S(1)}, bf16[18,1,192]{2,1,0:T(2,128)(2,1)S(1)}, u32[]{:S(2)}, u32[]{:S(2)}) %collective-permute-start.3) | collective-permute-done | bytes 6944 | tf_op jit(solution)/shard_map/ppermute | solution.py:32
  254.3 5.9 %all-to-all-start = ((bf16[16,32,192]{2,0,1:T(8,128)(2,1)}), bf16[16,32,192]{2,0,1:T(8,128)(2,1)S(1)}, u32[]{:S(2)}, u32[]{:S(2)}) async-start(bf16[16,32,192]{2,0,1:T(8,128)(2,1)} %copy.51), calls=%async_computation | async-start | bytes 524288 | tf_op jit(solution)/shard_map/all_to_all | solution.py:120
  260.7 0.9 fusion.52
  261.6 3.8 all-to-all-done
  265.5 0.9 fusion.38
  266.5 18.6 %all-reduce.27.cloned.1.call-done = f32[64,8,32]{2,1,0:T(8,128)} async-done(((f32[64,8,32]{2,1,0:T(8,128)}), f32[64,8,32]{2,1,0:T(8,128)}) %all-reduce.27.cloned.1.call-update) | async-done | bytes 65552 | tf_op jit(solution)/shard_map/psum | solution.py:79
  285.1 1.9 slice_bitcast_fusion.1
  287.0 1.2 copy.57
  288.2 76.2 %while.38 = (s32[]{:T(128)}, f32[16,64,8,192]{3,2,1,0:T(8,128)}, f32[16,64,8,1]{2,1,3,0:T(8,128)}, f32[64,8,192]{2,1,0:T(8,128)S(1)}, f32[16]{0:T(128)S(1)}, /*index=5*/f32[64,8,192]{2,1,0:T(8,128)S(1)}) while((s32[]{:T(128)}, f32[16,64,8,192]{3,2,1,0:T(8,128)}, f32[16,64,8,1]{2,1,3,0:T(8,128)}, f32[64,8,192]{2,1,0:T(8,128)S(1)}, ...), condition=%wide.region_9.10_spmd.clone, body=%wide.region_8.9_spmd.sunk.clone | while | flops 1035266 | bytes 11215489 | solution.py:68
  363.5 0.9 bitcast_dynamic-update-slice_fusion.7
  364.4 1.5 copy.53
  365.9 4.7 %multiply_reduce_fusion = f32[64,8,192]{2,1,0:T(8,128)S(1)} fusion(f32[16,64,8,192]{3,2,1,0:T(8,128)} %get-tuple-element.180, f32[64,8,192]{2,1,0:T(8,128)} %fusion.52, f32[16]{0:T(128)S(1)} %get-tuple-element.646, f32[16,64,8]{2,1,0:T(8,128)S(1)} %copy.53), kind=kLoop, calls=%fused_computation.69 | loop fusion | flops 7766016 | bytes 7110720 | tf_op jit(solution)/shard_map/reduce_sum | solution.py:75
  370.7 17.5 %all_to_all.52 = f32[64,8,192]{2,1,0:T(8,128)S(1)} all-to-all(f32[64,8,192]{2,1,0:T(8,128)S(1)} %multiply_add_fusion.9), channel_id=1, replica_groups=mesh['slides'=2,'rows'=4,'cols'=2,'chan'=2] {'rows'}, dimensions={0} | all-to-all | bytes 786432 | tf_op jit(solution)/shard_map/all_to_all | solution.py:130
  (1517 shorter events, 199.7 us)
Async XLA Ops:
  6.5 8.5 %copy-start = (f32[16,192]{1,0:T(8,128)S(1)}, f32[16,192]{1,0:T(8,128)}, u32[]{:S(2)}) copy-start(f32[16,192]{1,0:T(8,128)} %param.19) | copy-start | bytes 36868
  6.5 22.7 %all-reduce.25.cloned.1.call-start = ((), (), s32[]{:S(2)}) async-start(), calls=%async_computation.3 | async-start | bytes 524288 | tf_op jit(solution)/shard_map/psum | solution.py:97
  9.9 232.5 %all-to-all-start.1 = ((s32[4,1,128]{2,1,0:T(1,128)}), s32[4,1,128]{2,1,0:T(1,128)S(1)}, u32[]{:S(2)}, u32[]{:S(2)}) async-start(s32[4,1,128]{2,1,0:T(1,128)} %reshape.23), calls=%async_computation.1 | async-start | bytes 4096 | tf_op jit(solution)/shard_map/all_to_all | solution.py:121
  211.5 19.5 %copy-start.7 = (f32[16]{0:T(128)S(1)}, f32[16]{0:T(128)}, u32[]{:S(2)}) copy-start(f32[16]{0:T(128)} %get-tuple-element.644) | copy-start | bytes 196
  211.5 19.9 %copy-start.5 = (f32[16,16,32]{0,2,1:T(8,128)S(1)}, f32[16,16,32]{0,2,1:T(8,128)}, u32[]{:S(2)}) copy-start(f32[16,16,32]{0,2,1:T(8,128)} %get-tuple-element.321) | copy-start | bytes 98308
  211.5 20.0 %copy-start.4 = (f32[16,32,192]{2,1,0:T(8,128)S(1)}, f32[16,32,192]{2,1,0:T(8,128)}, u32[]{:S(2)}) copy-start(f32[16,32,192]{2,1,0:T(8,128)} %copy.49) | copy-start | bytes 1179652
  221.5 14.9 %copy-start.3 = (bf16[16,32,192]{2,1,0:T(8,128)(2,1)S(1)}, bf16[16,32,192]{2,1,0:T(8,128)(2,1)}, u32[]{:S(2)}) copy-start(bf16[16,32,192]{2,1,0:T(8,128)(2,1)} %param.16) | copy-start | bytes 589828
  221.5 14.9 %copy-start.10 = (f32[192]{0:T(256)S(1)}, f32[192]{0:T(256)}, u32[]{:S(2)}) copy-start(f32[192]{0:T(256)} %param.25) | copy-start | bytes 2308
  221.5 20.8 %copy-start.9 = (f32[3,3,192]{2,1,0:T(4,128)S(1)}, f32[3,3,192]{2,1,0:T(4,128)}, u32[]{:S(2)}) copy-start(f32[3,3,192]{2,1,0:T(4,128)} %param.23) | copy-start | bytes 20740
  231.0 21.9 %copy-start.11 = (f32[192]{0:T(256)S(1)}, f32[192]{0:T(256)}, u32[]{:S(2)}) copy-start(f32[192]{0:T(256)} %param.24) | copy-start | bytes 2308
  231.5 33.9 %copy-start.8 = (bf16[192,32]{0,1:T(8,128)(2,1)S(1)}, bf16[192,32]{0,1:T(8,128)(2,1)}, u32[]{:S(2)}) copy-start(bf16[192,32]{0,1:T(8,128)(2,1)} %param.22) | copy-start | bytes 36868
  236.5 7.2 %collective-permute-start = (bf16[1,32,192]{2,1,0:T(8,128)(2,1)S(1)}, bf16[1,32,192]{2,1,0:T(8,128)(2,1)S(1)}, u32[]{:S(2)}, u32[]{:S(2)}) collective-permute-start(bf16[1,32,192]{2,1,0:T(8,128)(2,1)S(1)} %get-tuple-element.319), channel_id=1, source_target_pairs={{0,4},{4,8},{8,12},{1,5},{5,9},{9,13},{2,6},{6,10},{10,14},{3,7},{... | collective-permute-start | bytes 36872 | tf_op jit(solution)/shard_map/ppermute | solution.py:29
  237.8 6.0 %collective-permute-start.1 = (bf16[1,32,192]{2,1,0:T(8,128)(2,1)S(1)}, bf16[1,32,192]{2,1,0:T(8,128)(2,1)S(1)}, u32[]{:S(2)}, u32[]{:S(2)}) collective-permute-start(bf16[1,32,192]{2,1,0:T(8,128)(2,1)S(1)} %get-tuple-element.320), channel_id=1, source_target_pairs={{4,0},{8,4},{12,8},{5,1},{9,5},{13,9},{6,2},{10,6},{14,10},{7,3},{... | collective-permute-start | bytes 36872 | tf_op jit(solution)/shard_map/ppermute | solution.py:32
  243.8 4.8 %collective-permute-start.2 = (bf16[18,1,192]{2,1,0:T(2,128)(2,1)S(1)}, bf16[18,1,192]{2,1,0:T(2,128)(2,1)S(1)}, u32[]{:S(2)}, u32[]{:S(2)}) collective-permute-start(bf16[18,1,192]{2,1,0:T(2,128)(2,1)S(1)} %get-tuple-element.315), channel_id=1, source_target_pairs={{0,2},{1,3},{4,6},{5,7},{8,10},{9,11},{12,14},{13,15},{16,18},{17,... | collective-permute-start | bytes 20744 | tf_op jit(solution)/shard_map/ppermute | solution.py:29
  247.2 5.7 %collective-permute-start.3 = (bf16[18,1,192]{2,1,0:T(2,128)(2,1)S(1)}, bf16[18,1,192]{2,1,0:T(2,128)(2,1)S(1)}, u32[]{:S(2)}, u32[]{:S(2)}) collective-permute-start(bf16[18,1,192]{2,1,0:T(2,128)(2,1)S(1)} %get-tuple-element.316), channel_id=1, source_target_pairs={{2,0},{3,1},{6,4},{7,5},{10,8},{11,9},{14,12},{15,13},{18,16},{19,... | collective-permute-start | bytes 20744 | tf_op jit(solution)/shard_map/ppermute | solution.py:32
  254.3 11.0 %all-to-all-start = ((bf16[16,32,192]{2,0,1:T(8,128)(2,1)}), bf16[16,32,192]{2,0,1:T(8,128)(2,1)S(1)}, u32[]{:S(2)}, u32[]{:S(2)}) async-start(bf16[16,32,192]{2,0,1:T(8,128)(2,1)} %copy.51), calls=%async_computation | async-start | bytes 524288 | tf_op jit(solution)/shard_map/all_to_all | solution.py:120
  260.3 24.8 %all-reduce.27.cloned.1.call-start = ((), (), s32[]{:S(2)}) async-start(), calls=%async_computation.4 | async-start | bytes 524288 | tf_op jit(solution)/shard_map/psum | solution.py:79
  265.5 22.7 %copy-start.1 = (bf16[16,4,8,192]{3,2,0,1:T(8,128)(2,1)}, bf16[16,4,8,192]{3,2,0,1:T(8,128)(2,1)S(1)}, u32[]{:S(2)}) copy-start(bf16[16,4,8,192]{3,2,0,1:T(8,128)(2,1)S(1)} %copy.52) | copy-start | bytes 589828
  364.4 6.2 %copy-start.2 = (bf16[16,4,8,192]{3,2,0,1:T(8,128)(2,1)S(1)}, bf16[16,4,8,192]{3,2,0,1:T(8,128)(2,1)}, u32[]{:S(2)}) copy-start(bf16[16,4,8,192]{3,2,0,1:T(8,128)(2,1)} %copy-done.1) | copy-start | bytes 589828
  364.4 23.8 %copy-start.6 = (bf16[16,32,192]{2,1,0:T(8,128)(2,1)S(1)}, bf16[16,32,192]{2,1,0:T(8,128)(2,1)}, u32[]{:S(2)}) copy-start(bf16[16,32,192]{2,1,0:T(8,128)(2,1)} %param.17) | copy-start | bytes 589828
Sparse Core Ops, SparseCore 0:
  9.7 19.4 all-reduce.24
  266.5 18.5 all-reduce.26
where the time goes:
time: 403 us; the launch traced here: 396 us
  local copies, waits for them, and re-layouts  178 us (44%)
  other arithmetic  104 us (26%)
  waiting for transfers between devices  32.1 us (8%)
  blocking collectives  31.4 us (8%)
  starting transfers between devices  21.5 us (5%)
  between operations  13.7 us (3%)
  loops' own time  10.1 us (3%)
  matrix products  4.34 us (1%)
    slice x464, local copies, waits for them, and re-layouts, one_state(): lax.associative_scan(combine_pair, (log_decays * state_scale, drive_col *...  66 us
    mul x32, other arithmetic, one_state(): log_decays * state_scale  41.8 us
    pad x288, local copies, waits for them, and re-layouts, one_state(): lax.associative_scan(combine_pair, (log_decays * state_scale, drive_col *...  36.8 us
    dynamic_slice x32, local copies, waits for them, and re-layouts, tile_states(): return (log_sums, lax.map(one_state, (state_rate, drive_cols)))  30.6 us
    dynamic_update_slice x32, other arithmetic, tile_states(): return (log_sums, lax.map(one_state, (state_rate, drive_cols)))  28.1 us
    mul x32, local copies, waits for them, and re-layouts, one_state(): drive_col * values  23.3 us
    psum x1, waiting for transfers between devices, column_coeffs(): lax.psum(jnp.dot(middle, proj_col, preferred_element_type=jnp.float32), '...  18.6 us
    all_to_all x1, blocking collectives, shards(): lax.all_to_all(strip_out, 'rows', split_axis=0, concat_axis=1, tiled=True)  17.5 us
  transfers between devices with their start and end apart: 8, of which 6 were waited for; matrix products, arithmetic and copies ran while one was open for 51% of the time, Pallas kernels for 0%

commit v1 on v0

v1 whole, which is shorter than its diff:
```python
import functools
import math

import jax
import jax.numpy as jnp
from jax import lax
from jax.experimental import pallas as pl
from jax.experimental.pallas import tpu as pltpu
from jax.sharding import PartitionSpec as P

MESH = pl.DeviceIdType.MESH
LANES = 128
GROUP = 8
PAD = 8
F32 = jnp.float32
BF16 = jnp.bfloat16
SIDES = ((-1, 0), (1, 0), (0, -1), (0, 1), (-1, -1), (-1, 1), (1, -1), (1, 1))


def opposite(side):
    return SIDES.index((-side[0], -side[1]))


def layer(
    dims,
    feats_ref,
    gate_ref,
    idx_ref,
    table_ref,
    rate_ref,
    proj_row_ref,
    proj_col_ref,
    conv_w_ref,
    conv_b_ref,
    skip_ref,
    out_ref,
    xf,
    lf,
    hot,
    cf,
    csend,
    crecv,
    ro,
    par,
    mb,
    rsend,
    rrecv,
    zsend,
    zrecv,
    edge_rows,
    edge_cols,
    got_rows,
    got_cols,
    coeff_sems,
    row_sems,
    col_sems,
    edge_sems,
):
    H, W, E, S, K, nz, nx = dims
    NT = -(-E // LANES)
    WP = W + 2 * PAD
    widths = [min(LANES, E - LANES * t) for t in range(NT)]
    z, x, c, sl = (lax.axis_index(a) for a in ("rows", "cols", "chan", "slides"))
    sibling = (sl, z, x, 1 - c)

    def exists(side):
        dz, dx = side
        parts = []
        if dz:
            parts.append(z > 0 if dz < 0 else z < nz - 1)
        if dx:
            parts.append(x > 0 if dx < 0 else x < nx - 1)
        return functools.reduce(jnp.logical_and, parts)

    def device(side):
        return (sl, z + side[0], x + side[1], c)

    barrier = pltpu.get_barrier_semaphore()
    pl.semaphore_signal(barrier, inc=1, device_id=sibling, device_id_type=MESH)
    for side in SIDES:

        @pl.when(exists(side))
        def _(side=side):
            pl.semaphore_signal(barrier, inc=1, device_id=device(side), device_id_type=MESH)

    flat = feats_ref[...].reshape(H * W, E)
    csend[0] = jnp.dot(flat, proj_row_ref[...], preferred_element_type=F32)
    peers_z = jnp.where(z > 0, 1, 0) + jnp.where(z < nz - 1, 1, 0)
    peers_x = jnp.where(x > 0, 1, 0) + jnp.where(x < nx - 1, 1, 0)
    pl.semaphore_wait(barrier, 1 + peers_z + peers_x + peers_z * peers_x)

    def coeff_copy(n):
        return pltpu.make_async_remote_copy(
            src_ref=csend.at[n],
            dst_ref=crecv.at[n],
            send_sem=coeff_sems.at[0, n],
            recv_sem=coeff_sems.at[1, n],
            device_id=sibling,
            device_id_type=MESH,
        )

    coeff_copy(0).start()

    for t in range(NT):
        w_t = widths[t]
        lo = t * LANES
        if w_t < LANES:
            xf[t] = jnp.zeros((H * W, LANES), F32)
            lf[t] = jnp.zeros((H * W, LANES), F32)
            par[t] = jnp.zeros((16, LANES), F32)
        xf[t, :, 0:w_t] = flat[:, lo : lo + w_t].astype(F32)
        for a in range(3):
            par[t, 3 * a : 3 * a + 3, 0:w_t] = conv_w_ref[a, :, lo : lo + w_t]
        par[t, 9:10, 0:w_t] = conv_b_ref[:, lo : lo + w_t]
        par[t, 10:11, 0:w_t] = skip_ref[:, lo : lo + w_t]
        ro[t] = jnp.zeros(((H + 2) * WP, LANES), F32)
    idx_t = idx_ref[...].astype(F32).T
    entry = lax.rem(lax.broadcasted_iota(jnp.int32, (W, 3 * K), 1), K).astype(F32)
    for h in range(H):
        hot[h * W : (h + 1) * W, :] = jnp.where(idx_t[:, h : h + 1] == entry, 1.0, 0.0)
    table = table_ref[...] * math.log2(math.e)
    first = table.astype(BF16)
    rest = table - first.astype(F32)
    second = rest.astype(BF16)
    third = (rest - second.astype(F32)).astype(BF16)
    logs = jnp.dot(
        hot[...].astype(BF16),
        jnp.concatenate([first, second, third], axis=0),
        preferred_element_type=F32,
    )
    for t in range(NT):
        lf[t, :, 0 : widths[t]] = logs[:, t * LANES : t * LANES + widths[t]]
    skips = [par[t, 10:11, :] for t in range(NT)]

    coeff_copy(0).wait()
    cf[:, 0 : 2 * S] = csend[0] + crecv[0]

    def scan_step(rows_at, states):
        coeffs = cf[rows_at, :]
        vals = [xf[t, rows_at, :] for t in range(NT)]
        logs_at = [lf[t, rows_at, :] for t in range(NT)]
        sums = [vals[t] * skips[t] for t in range(NT)]
        new = []
        for s in range(S):
            b = jnp.broadcast_to(coeffs[:, s : s + 1], (GROUP, LANES))
            o = jnp.broadcast_to(coeffs[:, S + s : S + s + 1], (GROUP, LANES))
            for t in range(NT):
                state = jnp.exp2(logs_at[t] * rate_ref[s]) * states[s * NT + t] + b * vals[t]
                sums[t] = sums[t] + o * state
                new.append(state)
        return sums, tuple(new)

    def carry_copy(send, recv, sems, n, side):
        return pltpu.make_async_remote_copy(
            src_ref=send.at[n],
            dst_ref=recv.at[n],
            send_sem=sems.at[0, n],
            recv_sem=sems.at[1, n],
            device_id=device(side),
            device_id_type=MESH,
        )

    def load_carry(recv, n):
        states = []
        for s in range(0, S, 2):
            pair = [recv[n, t, s * GROUP : (s + 2) * GROUP, :].astype(F32) for t in range(NT)]
            states += [p[:GROUP] for p in pair] + [p[GROUP:] for p in pair]
        return tuple(states)

    def store_carry(send, n, states):
        for t in range(NT):
            for s in range(0, S, 2):
                pair = jnp.concatenate([states[s * NT + t], states[(s + 1) * NT + t]], axis=0)
                send[n, t, s * GROUP : (s + 2) * GROUP, :] = pair.astype(BF16)

    @pl.when(x == 0)
    def _():
        rrecv[...] = jnp.zeros(rrecv.shape, BF16)

    for n in range(H // GROUP):

        @pl.when(x > 0)
        def _():
            carry_copy(rsend, rrecv, row_sems, n, (0, 1)).wait_recv()

        def row_step(w, states):
            sums, new = scan_step(pl.ds(n * GROUP * W + w, GROUP, stride=W), states)
            for t in range(NT):
                ro[t, pl.ds((n * GROUP + 1) * WP + PAD + w, GROUP, stride=WP), :] = (
                    sums[t].astype(BF16).astype(F32)
                )
            return new

        ends = lax.fori_loop(0, W, row_step, load_carry(rrecv, n))

        @pl.when(x < nx - 1)
        def _():
            store_carry(rsend, n, ends)
            carry_copy(rsend, rrecv, row_sems, n, (0, 1)).start()

    for t in range(NT):
        for n, h in enumerate((0, H - 1)):
            at = (h + 1) * WP + PAD
            edge_rows[n, t] = ro[t, at : at + W, :].astype(BF16)
        for n, w in enumerate((0, W - 1)):
            edge_cols[n, t] = ro[t, pl.ds(WP + PAD + w, H, stride=WP), :].astype(BF16)

    def edge_copy(k):
        dz, dx = SIDES[k]
        if dx == 0:
            src, dst = edge_rows.at[(dz + 1) // 2], got_rows.at[(1 - dz) // 2]
        else:
            src = edge_cols.at[(dx + 1) // 2]
            dst = got_cols.at[opposite(SIDES[k]) - 2]
        return pltpu.make_async_remote_copy(
            src_ref=src,
            dst_ref=dst,
            send_sem=edge_sems.at[0, k],
            recv_sem=edge_sems.at[1, opposite(SIDES[k])],
            device_id=device(SIDES[k]),
            device_id_type=MESH,
        )

    def edge_arrival(k):
        dz, dx = SIDES[k]
        buf = got_rows.at[(dz + 1) // 2] if dx == 0 else got_cols.at[k - 2]
        src = edge_rows.at[0] if dx == 0 else edge_cols.at[0]
        return pltpu.make_async_remote_copy(
            src_ref=src,
            dst_ref=buf,
            send_sem=edge_sems.at[0, k],
            recv_sem=edge_sems.at[1, k],
            device_id=device(SIDES[k]),
            device_id_type=MESH,
        )

    for k, side in enumerate(SIDES):

        @pl.when(exists(side))
        def _(k=k):
            edge_copy(k).start()

    for k, side in enumerate(SIDES):

        @pl.when(exists(side))
        def _(k=k, side=side):
            edge_arrival(k).wait_recv()
            dz, dx = side
            row = {-1: 0, 0: 1, 1: H + 1}[dz]
            col = {-1: PAD - 1, 0: PAD, 1: PAD + W}[dx]
            for t in range(NT):
                if dx == 0:
                    ro[t, row * WP + col : row * WP + col + W, :] = got_rows[
                        (dz + 1) // 2, t
                    ].astype(F32)
                elif dz == 0:
                    ro[t, pl.ds(row * WP + col, H, stride=WP), :] = got_cols[k - 2, t].astype(F32)
                else:
                    pick = H - 1 if dz < 0 else 0
                    ro[t, row * WP + col : row * WP + col + 1, :] = got_cols[k - 2, t].astype(F32)[
                        pick : pick + 1
                    ]

    def conv_step(h, unused):
        for t in range(NT):
            acc = jnp.broadcast_to(par[t, 9:10, :], (W, LANES))
            for a in range(3):
                for b in range(3):
                    start = (h + a) * WP
                    acc = acc + par[t, 3 * a + b : 3 * a + b + 1, :] * ro[
                        t, pl.ds(start + PAD - 1 + b, W), :
                    ]
            mid = (acc / (1.0 + jnp.exp(-acc))).astype(BF16)
            at = pl.ds(pl.multiple_of(h * W, W), W)
            xf[t, at, :] = mid.astype(F32)
            mb[at, t * LANES : t * LANES + widths[t]] = mid[:, 0 : widths[t]]
        return unused

    lax.fori_loop(0, H, conv_step, 0)

    csend[1] = jnp.dot(mb[...], proj_col_ref[...], preferred_element_type=F32)
    coeff_copy(1).start()
    coeff_copy(1).wait()
    cf[:, 0 : 2 * S] = csend[1] + crecv[1]

    @pl.when(z == 0)
    def _():
        zrecv[...] = jnp.zeros(zrecv.shape, BF16)

    for n in range(W // GROUP):

        @pl.when(z > 0)
        def _():
            carry_copy(zsend, zrecv, col_sems, n, (1, 0)).wait_recv()

        def col_step(h, states):
            at = pl.ds(pl.multiple_of(h * W + n * GROUP, GROUP), GROUP)
            sums, new = scan_step(at, states)
            for t in range(NT):
                xf[t, at, :] = sums[t]
            return new

        ends = lax.fori_loop(0, H, col_step, load_carry(zrecv, n))

        @pl.when(z < nz - 1)
        def _():
            store_carry(zsend, n, ends)
            carry_copy(zsend, zrecv, col_sems, n, (1, 0)).start()

    def gate_step(h, unused):
        at = pl.ds(pl.multiple_of(h * W, W), W)
        for t in range(NT):
            g = gate_ref[h, :, t * LANES : t * LANES + widths[t]].astype(F32)
            v = xf[t, at, 0 : widths[t]] * g / (1.0 + jnp.exp(-g))
            out_ref[h, :, t * LANES : t * LANES + widths[t]] = v.astype(BF16)
        return unused

    lax.fori_loop(0, H, gate_step, 0)

    for k, side in enumerate(SIDES):

        @pl.when(exists(side))
        def _(k=k):
            edge_copy(k).wait_send()

    @pl.when(x < nx - 1)
    def _():
        for n in range(H // GROUP):
            carry_copy(rsend, rrecv, row_sems, n, (0, 1)).wait_send()

    @pl.when(z < nz - 1)
    def _():
        for n in range(W // GROUP):
            carry_copy(zsend, zrecv, col_sems, n, (1, 0)).wait_send()


def shards(
    nz,
    nx,
    features,
    gate_input,
    decay_idx,
    log_table,
    state_rate,
    proj_row,
    proj_col,
    conv_w,
    conv_b,
    d_skip,
):
    H, W, E = features.shape
    S, K = state_rate.shape[0], log_table.shape[0]
    NT = -(-E // LANES)
    WP = W + 2 * PAD
    vmem = pl.BlockSpec(memory_space=pltpu.VMEM)
    smem = pl.BlockSpec(memory_space=pltpu.SMEM)
    dma = pltpu.SemaphoreType.DMA
    return pl.pallas_call(
        functools.partial(layer, (H, W, E, S, K, nz, nx)),
        out_shape=jax.ShapeDtypeStruct((H, W, E), BF16),
        in_specs=[vmem] * 4 + [smem] + [vmem] * 5,
        out_specs=vmem,
        scratch_shapes=[
            pltpu.VMEM((NT, H * W, LANES), F32),
            pltpu.VMEM((NT, H * W, LANES), F32),
            pltpu.VMEM((H * W, 3 * K), F32),
            pltpu.VMEM((H * W, LANES), F32),
            pltpu.VMEM((2, H * W, 2 * S), F32),
            pltpu.VMEM((2, H * W, 2 * S), F32),
            pltpu.VMEM((NT, (H + 2) * WP, LANES), F32),
            pltpu.VMEM((NT, 16, LANES), F32),
            pltpu.VMEM((H * W, E), BF16),
            pltpu.VMEM((H // GROUP, NT, S * GROUP, LANES), BF16),
            pltpu.VMEM((H // GROUP, NT, S * GROUP, LANES), BF16),
            pltpu.VMEM((W // GROUP, NT, S * GROUP, LANES), BF16),
            pltpu.VMEM((W // GROUP, NT, S * GROUP, LANES), BF16),
            pltpu.VMEM((2, NT, W, LANES), BF16),
            pltpu.VMEM((2, NT, H, LANES), BF16),
            pltpu.VMEM((2, NT, W, LANES), BF16),
            pltpu.VMEM((6, NT, H, LANES), BF16),
            dma((2, 2)),
            dma((2, H // GROUP)),
            dma((2, W // GROUP)),
            dma((2, 8)),
        ],
        compiler_params=pltpu.CompilerParams(
            collective_id=0, has_side_effects=True, vmem_limit_bytes=40 * 1024 * 1024
        ),
    )(
        features,
        gate_input,
        decay_idx,
        log_table,
        state_rate,
        proj_row,
        proj_col,
        conv_w,
        conv_b.reshape(1, E),
        d_skip.reshape(1, E),
    )


def solution(mesh):
    tile = P(("slides", "rows"), "cols", "chan")
    placed = (
        tile,
        tile,
        P(("slides", "rows"), "cols"),
        P(None, "chan"),
        P(),
        P("chan", None),
        P("chan", None),
        P(None, None, "chan"),
        P("chan"),
        P("chan"),
    )
    return jax.shard_map(
        functools.partial(shards, mesh.shape["rows"], mesh.shape["cols"]),
        mesh=mesh,
        in_specs=placed,
        out_specs=tile,
        check_vma=False,
    )
```

time: 403 us -> 55.7 us (0.14); the launches traced: 396 us -> 55.4 us
  local copies, waits for them, and re-layouts: 178 us -> 4.15 us
  other arithmetic: 104 us -> 0 us
  Pallas kernels: 0 us -> 51.1 us
  waiting for transfers between devices: 32.1 us -> 0 us
  blocking collectives: 31.4 us -> 0 us
  starting transfers between devices: 21.5 us -> 0 us
  between operations: 13.7 us -> 0.07 us
  loops' own time: 10.1 us -> 0 us
  matrix products: 4.34 us -> 0 us
    slice x468 -> x0, local copies, waits for them, and re-layouts: 66 us -> none  [the longest x464 66 us: one_state(): lax.associative_scan(combine_pair, (log_decays * state_scale, drive_col *...]
    pallas_call x0 -> x1, Pallas kernels: none -> 51.1 us  [shards(): pl.pallas_call(functools.partial(layer, (H, W, E, S, K, nz, nx)), out_sha...]
    mul x32 -> x0, other arithmetic: 41.8 us -> none  [one_state(): log_decays * state_scale]
    pad x288 -> x0, local copies, waits for them, and re-layouts: 36.8 us -> none  [one_state(): lax.associative_scan(combine_pair, (log_decays * state_scale, drive_col *...]
    dynamic_slice x32 -> x0, local copies, waits for them, and re-layouts: 30.6 us -> none  [tile_states(): return (log_sums, lax.map(one_state, (state_rate, drive_cols)))]
    dynamic_update_slice x32 -> x0, other arithmetic: 28.1 us -> none  [tile_states(): return (log_sums, lax.map(one_state, (state_rate, drive_cols)))]
    psum x2 -> x0, waiting for transfers between devices: 23.9 us -> none  [the longest x1 18.6 us: column_coeffs(): lax.psum(jnp.dot(middle, proj_col, preferred_element_type=jnp.float32), '...]
    mul x34 -> x0, local copies, waits for them, and re-layouts: 23.3 us -> none  [the longest x32 23.3 us: one_state(): drive_col * values]
  transfers between devices with their start and end apart: 8 -> 0, of which waited for: 6 -> 0; matrix products, arithmetic and copies ran while one was open for 51% -> 0% of each run, Pallas kernels for 0% -> 0%
where the time goes in v1:
time: 55.7 us; the launch traced here: 55.4 us
  Pallas kernels  51.1 us (92%)
  local copies, waits for them, and re-layouts  4.15 us (7%)
    pallas_call x1, Pallas kernels, shards(): pl.pallas_call(functools.partial(layer, (H, W, E, S, K, nz, nx)), out_sha...  51.1 us
    unnamed x21, local copies, waits for them, and re-layouts  4.15 us

profile of v1, /device:TPU:24, one launch (start us, length us, event | category | flops | bytes accessed | tf_op | source)
XLA Modules:
  0.0 55.4 jit_solution(2643306101264824747)
XLA Ops:
  0.0 0.0 copy-start.8
  0.0 0.8 %copy.11.proj_row_ref = bf16[192,32]{1,0:T(8,128)(2,1)S(1)} copy(bf16[192,32]{0,1:T(8,128)(2,1)} %param.15) | data formatting | bytes 24576 | tf_op args[5]
  0.8 0.0 copy-done.8
  0.9 0.0 copy-start.2
  0.9 0.0 copy-start.3
  0.9 0.0 copy-start.4
  0.9 0.0 copy-start.5
  0.9 0.0 copy-start.6
  0.9 0.0 copy-start.7
  0.9 0.1 copy.12.proj_col_ref
  1.0 0.5 copy-done.2
  1.6 0.0 copy-done.3
  1.6 0.0 copy-done.4
  1.6 0.0 copy-done.5
  1.6 0.0 copy-done.6
  1.6 0.0 copy-done.7
  1.6 0.0 copy-start
  1.6 0.9 %copy-done = bf16[16,32,192]{2,1,0:T(8,128)(2,1)S(1)} copy-done((bf16[16,32,192]{2,1,0:T(8,128)(2,1)S(1)}, bf16[16,32,192]{2,1,0:T(8,128)(2,1)}, u32[]{:S(2)}) %copy-start) | copy-done | bytes 196632
  2.6 0.0 copy-start.1
  2.6 0.9 %copy-done.1 = bf16[16,32,192]{2,1,0:T(8,128)(2,1)S(1)} copy-done((bf16[16,32,192]{2,1,0:T(8,128)(2,1)S(1)}, bf16[16,32,192]{2,1,0:T(8,128)(2,1)}, u32[]{:S(2)}) %copy-start.1) | copy-done | bytes 196632
  3.5 51.1 %shard_map.100 = bf16[16,32,192]{2,1,0:T(8,128)(2,1)S(1)} custom-call(bf16[16,32,192]{2,1,0:T(8,128)(2,1)S(1)} %copy-done, bf16[16,32,192]{2,1,0:T(8,128)(2,1)S(1)} %copy-done.1, s32[16,32]{1,0:T(8,128)S(1)} %copy-done.4, f32[16,192]{1,0:T(8,128)S(1)} %copy-done.2, f32[16]{0:T(128)S(1)} %copy-done.7, bf16[192,32]{1,0:T(8,128)(2,1)S(1)} %copy.11.proj_row_ref, ...), custom_call_target="tpu_custom_call" | custom-call | tf_op jit(solution)/shard_map/pallas_call | solution.py:358
  54.7 0.7 %copy.14 = bf16[16,32,192]{2,1,0:T(8,128)(2,1)} copy(bf16[16,32,192]{2,1,0:T(8,128)(2,1)S(1)} %shard_map.100) | data formatting | bytes 393216
Async XLA Ops:
  0.0 0.8 %copy-start.8 = (bf16[192,32]{0,1:T(8,128)(2,1)S(1)}, bf16[192,32]{0,1:T(8,128)(2,1)}, u32[]{:S(2)}) copy-start(bf16[192,32]{0,1:T(8,128)(2,1)} %param.16) | copy-start | bytes 36868
  0.9 0.7 %copy-start.2 = (f32[16,192]{1,0:T(8,128)S(1)}, f32[16,192]{1,0:T(8,128)}, u32[]{:S(2)}) copy-start(f32[16,192]{1,0:T(8,128)} %table_ref.1) | copy-start | bytes 36868
  0.9 0.7 %copy-start.3 = (f32[3,3,192]{2,1,0:T(4,128)S(1)}, f32[3,3,192]{2,1,0:T(4,128)}, u32[]{:S(2)}) copy-start(f32[3,3,192]{2,1,0:T(4,128)} %conv_w_ref.1) | copy-start | bytes 20740
  0.9 0.7 %copy-start.4 = (s32[16,32]{1,0:T(8,128)S(1)}, s32[16,32]{1,0:T(8,128)}, u32[]{:S(2)}) copy-start(s32[16,32]{1,0:T(8,128)} %idx_ref.1) | copy-start | bytes 6148
  0.9 0.7 %copy-start.5 = (f32[192]{0:T(256)S(1)}, f32[192]{0:T(256)}, u32[]{:S(2)}) copy-start(f32[192]{0:T(256)} %param.18) | copy-start | bytes 2308
  0.9 0.7 %copy-start.6 = (f32[192]{0:T(256)S(1)}, f32[192]{0:T(256)}, u32[]{:S(2)}) copy-start(f32[192]{0:T(256)} %param.19) | copy-start | bytes 2308
  0.9 0.7 %copy-start.7 = (f32[16]{0:T(128)S(1)}, f32[16]{0:T(128)}, u32[]{:S(2)}) copy-start(f32[16]{0:T(128)} %rate_ref.1) | copy-start | bytes 196
  1.6 1.0 %copy-start = (bf16[16,32,192]{2,1,0:T(8,128)(2,1)S(1)}, bf16[16,32,192]{2,1,0:T(8,128)(2,1)}, u32[]{:S(2)}) copy-start(bf16[16,32,192]{2,1,0:T(8,128)(2,1)} %feats_ref.1) | copy-start | bytes 589828
  2.6 0.9 %copy-start.1 = (bf16[16,32,192]{2,1,0:T(8,128)(2,1)S(1)}, bf16[16,32,192]{2,1,0:T(8,128)(2,1)}, u32[]{:S(2)}) copy-start(bf16[16,32,192]{2,1,0:T(8,128)(2,1)} %gate_ref.1) | copy-start | bytes 589828

commit v2 on v1

--- a/solution.py
+++ b/solution.py
@@ -12,6 +12,8 @@
 LANES = 128
 GROUP = 8
 PAD = 8
+SPLIT = 2
+UNROLL = 16
 F32 = jnp.float32
 BF16 = jnp.bfloat16
 SIDES = ((-1, 0), (1, 0), (0, -1), (0, 1), (-1, -1), (-1, 1), (1, -1), (1, 1))
@@ -21,10 +23,14 @@
     return SIDES.index((-side[0], -side[1]))
 
 
+def project(vals, proj_t):
+    return lax.dot_general(vals, proj_t, (((1,), (1,)), ((), ())), preferred_element_type=F32)
+
+
 def layer(
     dims,
-    feats_ref,
-    gate_ref,
+    feats_hbm,
+    gate_hbm,
     idx_ref,
     table_ref,
     rate_ref,
@@ -34,7 +40,10 @@
     conv_b_ref,
     skip_ref,
     out_ref,
+    feats_ref,
+    gate_ref,
     xf,
+    yf,
     lf,
     hot,
     cf,
@@ -55,6 +64,7 @@
     row_sems,
     col_sems,
     edge_sems,
+    load_sems,
 ):
     H, W, E, S, K, nz, nx = dims
     NT = -(-E // LANES)
@@ -75,6 +85,10 @@
     def device(side):
         return (sl, z + side[0], x + side[1], c)
 
+    feats_load = pltpu.make_async_copy(feats_hbm, feats_ref, load_sems.at[0])
+    gate_load = pltpu.make_async_copy(gate_hbm, gate_ref, load_sems.at[1])
+    feats_load.start()
+    gate_load.start()
     barrier = pltpu.get_barrier_semaphore()
     pl.semaphore_signal(barrier, inc=1, device_id=sibling, device_id_type=MESH)
     for side in SIDES:
@@ -83,8 +97,9 @@
         def _(side=side):
             pl.semaphore_signal(barrier, inc=1, device_id=device(side), device_id_type=MESH)
 
+    feats_load.wait()
     flat = feats_ref[...].reshape(H * W, E)
-    csend[0] = jnp.dot(flat, proj_row_ref[...], preferred_element_type=F32)
+    csend[0] = project(flat, proj_row_ref[...])
     peers_z = jnp.where(z > 0, 1, 0) + jnp.where(z < nz - 1, 1, 0)
     peers_x = jnp.where(x > 0, 1, 0) + jnp.where(x < nx - 1, 1, 0)
     pl.semaphore_wait(barrier, 1 + peers_z + peers_x + peers_z * peers_x)
@@ -135,17 +150,23 @@
     coeff_copy(0).wait()
     cf[:, 0 : 2 * S] = csend[0] + crecv[0]
 
-    def scan_step(rows_at, states):
+    SQ = S // SPLIT
+    packed = widths[-1] <= LANES // 2
+    low_lanes = lax.broadcasted_iota(jnp.int32, (GROUP, LANES), 1) < LANES // 2
+
+    def scan_step(rows_at, q, sums, states):
         coeffs = cf[rows_at, :]
         vals = [xf[t, rows_at, :] for t in range(NT)]
         logs_at = [lf[t, rows_at, :] for t in range(NT)]
-        sums = [vals[t] * skips[t] for t in range(NT)]
+        if q == 0:
+            sums = [vals[t] * skips[t] for t in range(NT)]
         new = []
-        for s in range(S):
+        for k in range(SQ):
+            s = q * SQ + k
             b = jnp.broadcast_to(coeffs[:, s : s + 1], (GROUP, LANES))
             o = jnp.broadcast_to(coeffs[:, S + s : S + s + 1], (GROUP, LANES))
             for t in range(NT):
-                state = jnp.exp2(logs_at[t] * rate_ref[s]) * states[s * NT + t] + b * vals[t]
+                state = jnp.exp2(logs_at[t] * rate_ref[s]) * states[k * NT + t] + b * vals[t]
                 sums[t] = sums[t] + o * state
                 new.append(state)
         return sums, tuple(new)
@@ -160,43 +181,66 @@
             device_id_type=MESH,
         )
 
+    def half_turn(v):
+        return pltpu.roll(v, LANES // 2, axis=1)
+
     def load_carry(recv, n):
-        states = []
-        for s in range(0, S, 2):
-            pair = [recv[n, t, s * GROUP : (s + 2) * GROUP, :].astype(F32) for t in range(NT)]
-            states += [p[:GROUP] for p in pair] + [p[GROUP:] for p in pair]
+        states = [None] * (SQ * NT)
+        at = 0
+        for t in range(NT):
+            tail = packed and t == NT - 1
+            for k in range(0, SQ, 4 if tail else 2):
+                pair = recv[n, at : at + 2 * GROUP, :].astype(F32)
+                at += 2 * GROUP
+                for i in range(2):
+                    v = pair[i * GROUP : (i + 1) * GROUP]
+                    if tail:
+                        states[(k + 2 * i) * NT + t] = jnp.where(low_lanes, v, 0.0)
+                        states[(k + 2 * i + 1) * NT + t] = jnp.where(low_lanes, half_turn(v), 0.0)
+                    else:
+                        states[(k + i) * NT + t] = v
         return tuple(states)
 
     def store_carry(send, n, states):
+        at = 0
         for t in range(NT):
-            for s in range(0, S, 2):
-                pair = jnp.concatenate([states[s * NT + t], states[(s + 1) * NT + t]], axis=0)
-                send[n, t, s * GROUP : (s + 2) * GROUP, :] = pair.astype(BF16)
+            tail = packed and t == NT - 1
+            own = [states[k * NT + t] for k in range(SQ)]
+            if tail:
+                own = [own[k] + half_turn(own[k + 1]) for k in range(0, SQ, 2)]
+            for k in range(0, len(own), 2):
+                pair = jnp.concatenate([own[k], own[k + 1]], axis=0)
+                send[n, at : at + 2 * GROUP, :] = pair.astype(BF16)
+                at += 2 * GROUP
 
     @pl.when(x == 0)
     def _():
         rrecv[...] = jnp.zeros(rrecv.shape, BF16)
 
     for n in range(H // GROUP):
-
-        @pl.when(x > 0)
-        def _():
-            carry_copy(rsend, rrecv, row_sems, n, (0, 1)).wait_recv()
-
-        def row_step(w, states):
-            sums, new = scan_step(pl.ds(n * GROUP * W + w, GROUP, stride=W), states)
-            for t in range(NT):
-                ro[t, pl.ds((n * GROUP + 1) * WP + PAD + w, GROUP, stride=WP), :] = (
-                    sums[t].astype(BF16).astype(F32)
-                )
-            return new
-
-        ends = lax.fori_loop(0, W, row_step, load_carry(rrecv, n))
-
-        @pl.when(x < nx - 1)
-        def _():
-            store_carry(rsend, n, ends)
-            carry_copy(rsend, rrecv, row_sems, n, (0, 1)).start()
+        for q in range(SPLIT):
+            m = n * SPLIT + q
+
+            @pl.when(x > 0)
+            def _():
+                carry_copy(rsend, rrecv, row_sems, m, (0, 1)).wait_recv()
+
+            def row_step(w, states):
+                to = pl.ds((n * GROUP + 1) * WP + PAD + w, GROUP, stride=WP)
+                sums = [ro[t, to, :] for t in range(NT)] if q else None
+                at = pl.ds(n * GROUP * W + w, GROUP, stride=W)
+                sums, new = scan_step(at, q, sums, states)
+                for t in range(NT):
+                    last = q == SPLIT - 1
+                    ro[t, to, :] = sums[t].astype(BF16).astype(F32) if last else sums[t]
+                return new
+
+            ends = lax.fori_loop(0, W, row_step, load_carry(rrecv, m), unroll=UNROLL)
+
+            @pl.when(x < nx - 1)
+            def _():
+                store_carry(rsend, m, ends)
+                carry_copy(rsend, rrecv, row_sems, m, (0, 1)).start()
 
     for t in range(NT):
         for n, h in enumerate((0, H - 1)):
@@ -276,9 +320,9 @@
             mb[at, t * LANES : t * LANES + widths[t]] = mid[:, 0 : widths[t]]
         return unused
 
-    lax.fori_loop(0, H, conv_step, 0)
-
-    csend[1] = jnp.dot(mb[...], proj_col_ref[...], preferred_element_type=F32)
+    lax.fori_loop(0, H, conv_step, 0, unroll=4)
+
+    csend[1] = project(mb[...], proj_col_ref[...])
     coeff_copy(1).start()
     coeff_copy(1).wait()
     cf[:, 0 : 2 * S] = csend[1] + crecv[1]
@@ -288,34 +332,38 @@
         zrecv[...] = jnp.zeros(zrecv.shape, BF16)
 
     for n in range(W // GROUP):
-
-        @pl.when(z > 0)
-        def _():
-            carry_copy(zsend, zrecv, col_sems, n, (1, 0)).wait_recv()
-
-        def col_step(h, states):
-            at = pl.ds(pl.multiple_of(h * W + n * GROUP, GROUP), GROUP)
-            sums, new = scan_step(at, states)
-            for t in range(NT):
-                xf[t, at, :] = sums[t]
-            return new
-
-        ends = lax.fori_loop(0, H, col_step, load_carry(zrecv, n))
-
-        @pl.when(z < nz - 1)
-        def _():
-            store_carry(zsend, n, ends)
-            carry_copy(zsend, zrecv, col_sems, n, (1, 0)).start()
-
+        for q in range(SPLIT):
+            m = n * SPLIT + q
+
+            @pl.when(z > 0)
+            def _():
+                carry_copy(zsend, zrecv, col_sems, m, (1, 0)).wait_recv()
+
+            def col_step(h, states):
+                at = pl.ds(pl.multiple_of(h * W + n * GROUP, GROUP), GROUP)
+                sums = [yf[t, at, :] for t in range(NT)] if q else None
+                sums, new = scan_step(at, q, sums, states)
+                for t in range(NT):
+                    yf[t, at, :] = sums[t]
+                return new
+
+            ends = lax.fori_loop(0, H, col_step, load_carry(zrecv, m), unroll=UNROLL)
+
+            @pl.when(z < nz - 1)
+            def _():
+                store_carry(zsend, m, ends)
+                carry_copy(zsend, zrecv, col_sems, m, (1, 0)).start()
+
+    gate_load.wait()
     def gate_step(h, unused):
         at = pl.ds(pl.multiple_of(h * W, W), W)
         for t in range(NT):
             g = gate_ref[h, :, t * LANES : t * LANES + widths[t]].astype(F32)
-            v = xf[t, at, 0 : widths[t]] * g / (1.0 + jnp.exp(-g))
+            v = yf[t, at, 0 : widths[t]] * g / (1.0 + jnp.exp(-g))
             out_ref[h, :, t * LANES : t * LANES + widths[t]] = v.astype(BF16)
         return unused
 
-    lax.fori_loop(0, H, gate_step, 0)
+    lax.fori_loop(0, H, gate_step, 0, unroll=4)
 
     for k, side in enumerate(SIDES):
 
@@ -325,12 +373,12 @@
 
     @pl.when(x < nx - 1)
     def _():
-        for n in range(H // GROUP):
+        for n in range(H // GROUP * SPLIT):
             carry_copy(rsend, rrecv, row_sems, n, (0, 1)).wait_send()
 
     @pl.when(z < nz - 1)
     def _():
-        for n in range(W // GROUP):
+        for n in range(W // GROUP * SPLIT):
             carry_copy(zsend, zrecv, col_sems, n, (1, 0)).wait_send()
 
 
@@ -352,15 +400,21 @@
     S, K = state_rate.shape[0], log_table.shape[0]
     NT = -(-E // LANES)
     WP = W + 2 * PAD
+    tail = E - (NT - 1) * LANES
+    depth = (2 * NT - (tail <= LANES // 2)) * (S // SPLIT) * GROUP // 2
     vmem = pl.BlockSpec(memory_space=pltpu.VMEM)
+    hbm = pl.BlockSpec(memory_space=pl.ANY)
     smem = pl.BlockSpec(memory_space=pltpu.SMEM)
     dma = pltpu.SemaphoreType.DMA
     return pl.pallas_call(
         functools.partial(layer, (H, W, E, S, K, nz, nx)),
         out_shape=jax.ShapeDtypeStruct((H, W, E), BF16),
-        in_specs=[vmem] * 4 + [smem] + [vmem] * 5,
+        in_specs=[hbm] * 2 + [vmem] * 2 + [smem] + [vmem] * 5,
         out_specs=vmem,
         scratch_shapes=[
+            pltpu.VMEM((H, W, E), BF16),
+            pltpu.VMEM((H, W, E), BF16),
+            pltpu.VMEM((NT, H * W, LANES), F32),
             pltpu.VMEM((NT, H * W, LANES), F32),
             pltpu.VMEM((NT, H * W, LANES), F32),
             pltpu.VMEM((H * W, 3 * K), F32),
@@ -370,21 +424,22 @@
             pltpu.VMEM((NT, (H + 2) * WP, LANES), F32),
             pltpu.VMEM((NT, 16, LANES), F32),
             pltpu.VMEM((H * W, E), BF16),
-            pltpu.VMEM((H // GROUP, NT, S * GROUP, LANES), BF16),
-            pltpu.VMEM((H // GROUP, NT, S * GROUP, LANES), BF16),
-            pltpu.VMEM((W // GROUP, NT, S * GROUP, LANES), BF16),
-            pltpu.VMEM((W // GROUP, NT, S * GROUP, LANES), BF16),
+            pltpu.VMEM((H // GROUP * SPLIT, depth, LANES), BF16),
+            pltpu.VMEM((H // GROUP * SPLIT, depth, LANES), BF16),
+            pltpu.VMEM((W // GROUP * SPLIT, depth, LANES), BF16),
+            pltpu.VMEM((W // GROUP * SPLIT, depth, LANES), BF16),
             pltpu.VMEM((2, NT, W, LANES), BF16),
             pltpu.VMEM((2, NT, H, LANES), BF16),
             pltpu.VMEM((2, NT, W, LANES), BF16),
             pltpu.VMEM((6, NT, H, LANES), BF16),
             dma((2, 2)),
-            dma((2, H // GROUP)),
-            dma((2, W // GROUP)),
+            dma((2, H // GROUP * SPLIT)),
+            dma((2, W // GROUP * SPLIT)),
             dma((2, 8)),
+            dma((2,)),
         ],
         compiler_params=pltpu.CompilerParams(
-            collective_id=0, has_side_effects=True, vmem_limit_bytes=40 * 1024 * 1024
+            collective_id=0, has_side_effects=True, vmem_limit_bytes=60 * 1024 * 1024
         ),
     )(
         features,
@@ -392,8 +447,8 @@
         decay_idx,
         log_table,
         state_rate,
-        proj_row,
-        proj_col,
+        proj_row.T,
+        proj_col.T,
         conv_w,
         conv_b.reshape(1, E),
         d_skip.reshape(1, E),

time: 55.7 us -> 36.7 us (0.66)
  Pallas kernels: 51.1 us -> 34.8 us
  local copies, waits for them, and re-layouts: 4.15 us -> 1.67 us
    pallas_call x1, Pallas kernels: 51.1 us -> 34.8 us  [shards(): pl.pallas_call(functools.partial(layer, (H, W, E, S, K, nz, nx)), out_sha...]
    unnamed x21 -> x1, local copies, waits for them, and re-layouts: 4.15 us -> 1.67 us
where the time goes in v2:
time: 36.7 us; the launch traced here: 36.5 us
  Pallas kernels  34.8 us (95%)
  local copies, waits for them, and re-layouts  1.67 us (5%)
    pallas_call x1, Pallas kernels, shards(): pl.pallas_call(functools.partial(layer, (H, W, E, S, K, nz, nx)), out_sha...  34.8 us
    unnamed x1, local copies, waits for them, and re-layouts  1.67 us

profile of v2, /device:TPU:24, one launch (start us, length us, event | category | flops | bytes accessed | tf_op | source)
XLA Modules:
  0.0 36.5 jit_solution(1520938626326926367)
XLA Ops:
  0.0 34.8 %shard_map.100 = bf16[16,32,192]{2,1,0:T(8,128)(2,1)} custom-call(bf16[16,32,192]{2,1,0:T(8,128)(2,1)} %feats_hbm.1, bf16[16,32,192]{2,1,0:T(8,128)(2,1)} %gate_hbm.1, s32[16,32]{1,0:T(8,128)} %idx_ref.1, f32[16,192]{1,0:T(8,128)} %table_ref.1, f32[16]{0:T(128)} %rate_ref.1, bf16[32,192]{1,0:T(8,128)(2,1)} %bitcast.4, bf16[32,192]{1,0:T(8,128)(2,1)} %bitcast.5, ...), custom_call_target="tpu_custom_call" | custom-call | tf_op jit(solution)/shard_map/pallas_call | solution.py:409
  34.8 1.7 %copy.12 = bf16[16,32,192]{2,1,0:T(8,128)(2,1)} copy(bf16[16,32,192]{2,1,0:T(8,128)(2,1)} %shard_map.100) | data formatting | bytes 393216

commit v3 on v2

--- a/solution.py
+++ b/solution.py
@@ -12,8 +12,10 @@
 LANES = 128
 GROUP = 8
 PAD = 8
-SPLIT = 2
-UNROLL = 16
+ROW_SPLIT = 2
+COL_SPLIT = 4
+ROW_UNROLL = 32
+COL_UNROLL = 16
 F32 = jnp.float32
 BF16 = jnp.bfloat16
 SIDES = ((-1, 0), (1, 0), (0, -1), (0, 1), (-1, -1), (-1, 1), (1, -1), (1, 1))
@@ -150,11 +152,11 @@
     coeff_copy(0).wait()
     cf[:, 0 : 2 * S] = csend[0] + crecv[0]
 
-    SQ = S // SPLIT
     packed = widths[-1] <= LANES // 2
     low_lanes = lax.broadcasted_iota(jnp.int32, (GROUP, LANES), 1) < LANES // 2
 
     def scan_step(rows_at, q, sums, states):
+        SQ = len(states) // NT
         coeffs = cf[rows_at, :]
         vals = [xf[t, rows_at, :] for t in range(NT)]
         logs_at = [lf[t, rows_at, :] for t in range(NT)]
@@ -184,7 +186,7 @@
     def half_turn(v):
         return pltpu.roll(v, LANES // 2, axis=1)
 
-    def load_carry(recv, n):
+    def load_carry(recv, n, SQ):
         states = [None] * (SQ * NT)
         at = 0
         for t in range(NT):
@@ -202,6 +204,7 @@
         return tuple(states)
 
     def store_carry(send, n, states):
+        SQ = len(states) // NT
         at = 0
         for t in range(NT):
             tail = packed and t == NT - 1
@@ -218,8 +221,8 @@
         rrecv[...] = jnp.zeros(rrecv.shape, BF16)
 
     for n in range(H // GROUP):
-        for q in range(SPLIT):
-            m = n * SPLIT + q
+        for q in range(ROW_SPLIT):
+            m = n * ROW_SPLIT + q
 
             @pl.when(x > 0)
             def _():
@@ -231,11 +234,11 @@
                 at = pl.ds(n * GROUP * W + w, GROUP, stride=W)
                 sums, new = scan_step(at, q, sums, states)
                 for t in range(NT):
-                    last = q == SPLIT - 1
+                    last = q == ROW_SPLIT - 1
                     ro[t, to, :] = sums[t].astype(BF16).astype(F32) if last else sums[t]
                 return new
 
-            ends = lax.fori_loop(0, W, row_step, load_carry(rrecv, m), unroll=UNROLL)
+            ends = lax.fori_loop(0, W, row_step, load_carry(rrecv, m, S // ROW_SPLIT), unroll=ROW_UNROLL)
 
             @pl.when(x < nx - 1)
             def _():
@@ -284,10 +287,10 @@
         def _(k=k):
             edge_copy(k).start()
 
-    for k, side in enumerate(SIDES):
+    def arrive(k, side):
 
         @pl.when(exists(side))
-        def _(k=k, side=side):
+        def _():
             edge_arrival(k).wait_recv()
             dz, dx = side
             row = {-1: 0, 0: 1, 1: H + 1}[dz]
@@ -320,7 +323,15 @@
             mb[at, t * LANES : t * LANES + widths[t]] = mid[:, 0 : widths[t]]
         return unused
 
-    lax.fori_loop(0, H, conv_step, 0, unroll=4)
+    across = [k for k, side in enumerate(SIDES) if side[0] == 0]
+    for k in across:
+        arrive(k, SIDES[k])
+    lax.fori_loop(1, H - 1, conv_step, 0, unroll=2 - H % 2)
+    for k, side in enumerate(SIDES):
+        if k not in across:
+            arrive(k, side)
+    for h in (0, H - 1):
+        conv_step(h, 0)
 
     csend[1] = project(mb[...], proj_col_ref[...])
     coeff_copy(1).start()
@@ -332,8 +343,8 @@
         zrecv[...] = jnp.zeros(zrecv.shape, BF16)
 
     for n in range(W // GROUP):
-        for q in range(SPLIT):
-            m = n * SPLIT + q
+        for q in range(COL_SPLIT):
+            m = n * COL_SPLIT + q
 
             @pl.when(z > 0)
             def _():
@@ -347,7 +358,7 @@
                     yf[t, at, :] = sums[t]
                 return new
 
-            ends = lax.fori_loop(0, H, col_step, load_carry(zrecv, m), unroll=UNROLL)
+            ends = lax.fori_loop(0, H, col_step, load_carry(zrecv, m, S // COL_SPLIT), unroll=COL_UNROLL)
 
             @pl.when(z < nz - 1)
             def _():
@@ -373,12 +384,12 @@
 
     @pl.when(x < nx - 1)
     def _():
-        for n in range(H // GROUP * SPLIT):
+        for n in range(H // GROUP * ROW_SPLIT):
             carry_copy(rsend, rrecv, row_sems, n, (0, 1)).wait_send()
 
     @pl.when(z < nz - 1)
     def _():
-        for n in range(W // GROUP * SPLIT):
+        for n in range(W // GROUP * COL_SPLIT):
             carry_copy(zsend, zrecv, col_sems, n, (1, 0)).wait_send()
 
 
@@ -401,7 +412,7 @@
     NT = -(-E // LANES)
     WP = W + 2 * PAD
     tail = E - (NT - 1) * LANES
-    depth = (2 * NT - (tail <= LANES // 2)) * (S // SPLIT) * GROUP // 2
+    depth = (2 * NT - (tail <= LANES // 2)) * S * GROUP // 2
     vmem = pl.BlockSpec(memory_space=pltpu.VMEM)
     hbm = pl.BlockSpec(memory_space=pl.ANY)
     smem = pl.BlockSpec(memory_space=pltpu.SMEM)
@@ -424,17 +435,17 @@
             pltpu.VMEM((NT, (H + 2) * WP, LANES), F32),
             pltpu.VMEM((NT, 16, LANES), F32),
             pltpu.VMEM((H * W, E), BF16),
-            pltpu.VMEM((H // GROUP * SPLIT, depth, LANES), BF16),
-            pltpu.VMEM((H // GROUP * SPLIT, depth, LANES), BF16),
-            pltpu.VMEM((W // GROUP * SPLIT, depth, LANES), BF16),
-            pltpu.VMEM((W // GROUP * SPLIT, depth, LANES), BF16),
+            pltpu.VMEM((H // GROUP * ROW_SPLIT, depth // ROW_SPLIT, LANES), BF16),
+            pltpu.VMEM((H // GROUP * ROW_SPLIT, depth // ROW_SPLIT, LANES), BF16),
+            pltpu.VMEM((W // GROUP * COL_SPLIT, depth // COL_SPLIT, LANES), BF16),
+            pltpu.VMEM((W // GROUP * COL_SPLIT, depth // COL_SPLIT, LANES), BF16),
             pltpu.VMEM((2, NT, W, LANES), BF16),
             pltpu.VMEM((2, NT, H, LANES), BF16),
             pltpu.VMEM((2, NT, W, LANES), BF16),
             pltpu.VMEM((6, NT, H, LANES), BF16),
             dma((2, 2)),
-            dma((2, H // GROUP * SPLIT)),
-            dma((2, W // GROUP * SPLIT)),
+            dma((2, H // GROUP * ROW_SPLIT)),
+            dma((2, W // GROUP * COL_SPLIT)),
             dma((2, 8)),
             dma((2,)),
         ],

time: 36.7 us -> 34.9 us (0.951)
  Pallas kernels: 34.8 us -> 33 us
    pallas_call x1, Pallas kernels: 34.8 us -> 33 us  [shards(): pl.pallas_call(functools.partial(layer, (H, W, E, S, K, nz, nx)), out_sha...]
where the time goes in v3:
time: 34.9 us; the launch traced here: 34.7 us
  Pallas kernels  33 us (95%)
  local copies, waits for them, and re-layouts  1.67 us (5%)
    pallas_call x1, Pallas kernels, shards(): pl.pallas_call(functools.partial(layer, (H, W, E, S, K, nz, nx)), out_sha...  33 us
    unnamed x1, local copies, waits for them, and re-layouts  1.67 us

profile of v3, /device:TPU:24, one launch (start us, length us, event | category | flops | bytes accessed | tf_op | source)
XLA Modules:
  0.0 34.7 jit_solution(13470183420922091095)
XLA Ops:
  0.0 33.0 %shard_map.100 = bf16[16,32,192]{2,1,0:T(8,128)(2,1)} custom-call(bf16[16,32,192]{2,1,0:T(8,128)(2,1)} %feats_hbm.1, bf16[16,32,192]{2,1,0:T(8,128)(2,1)} %gate_hbm.1, s32[16,32]{1,0:T(8,128)} %idx_ref.1, f32[16,192]{1,0:T(8,128)} %table_ref.1, f32[16]{0:T(128)} %rate_ref.1, bf16[32,192]{1,0:T(8,128)(2,1)} %bitcast.4, bf16[32,192]{1,0:T(8,128)(2,1)} %bitcast.5, ...), custom_call_target="tpu_custom_call" | custom-call | tf_op jit(solution)/shard_map/pallas_call | solution.py:420
  33.0 1.7 %copy.12 = bf16[16,32,192]{2,1,0:T(8,128)(2,1)} copy(bf16[16,32,192]{2,1,0:T(8,128)(2,1)} %shard_map.100) | data formatting | bytes 393216
